TPU v7x, 32 devices: a whole 2x2x4 slice. The times are simulated.
32 devices in a mesh: space: 2 (over core), chan: 16 (over z, y, x).
Axes of the slice: x: 2, y: 2, z: 4, core: 2. Of those that a mesh axis runs over, the one named last changes fastest.
Arguments:
- acts: bfloat16 [256, 128, 4096], P('chan', 'space'), may hold values from -6 to 6
- w_point: bfloat16 [256, 256], replicated, may hold values from -0.375 to 0.375
- w_tap: bfloat16 [8, 256, 256], replicated, may hold values from -0.125 to 0.125
- grad_out: bfloat16 [256, 64, 1024], P('chan', 'space'), may hold values from -6 to 6
Outputs:
- out_map: bfloat16 [256, 64, 1024], P(None, ('space', 'chan'))
- d_acts: bfloat16 [256, 128, 4096], P(None, ('space', 'chan'))
- d_point: float32 [256, 256], P('chan', 'space')
- d_tap: float32 [8, 256, 256], P(None, 'chan', 'space')
All inputs are finite; a program needn't handle non-finite values.
Results may differ from a plain program's by a relative error of at most 0.0049.
Values may be sent and summed in bfloat16 or wider, within the bound.
A program may use at most 128 MiB of HBM per device.

v0:
```python
import math

import jax
import jax.numpy as jnp
from jax import lax
from jax.sharding import PartitionSpec as P

H = 64
W = 64


def gelu_tanh(value):
    return jax.nn.gelu(value, approximate=True)


def spread_blocks(partial_value, space_count, chan_count):
    lead_count, channels, filters = partial_value.shape
    blocks = partial_value.reshape(
        lead_count, chan_count, channels // chan_count, space_count, filters // space_count
    )
    blocks = jnp.transpose(blocks, (3, 1, 0, 2, 4))
    return blocks.reshape(
        space_count * chan_count, lead_count, channels // chan_count, filters // space_count
    )


def shards(acts, w_point, w_tap, grad_out):
    space_count = lax.axis_size("space")
    chan_count = lax.axis_size("chan")
    inputs = lax.all_to_all(acts, "chan", split_axis=1, concat_axis=0, tiled=True)
    channels = inputs.shape[0]
    row_count = inputs.shape[1]
    filters = w_tap.shape[2]
    in_cells = row_count * chan_count * space_count * H * W
    in_scale = 1.0 / math.sqrt(in_cells)
    out_scale = 1.0 / math.sqrt(in_cells // 8)
    pre_act = jnp.einsum("cd,crp->drp", w_point, inputs, preferred_element_type=jnp.float32)
    hidden_full, gelu_back = jax.vjp(gelu_tanh, pre_act)
    hidden = hidden_full.astype(jnp.bfloat16)
    hidden_cube = hidden.reshape(channels, row_count // 2, 2, H // 2, 2, W // 2, 2)
    tap_weights = w_tap.reshape(2, 2, 2, channels, filters)
    output = jnp.einsum(
        "abedf,dqaibje->fqij", tap_weights, hidden_cube, preferred_element_type=jnp.float32
    )
    out_map = output.reshape(filters, row_count // 2, H // 2 * (W // 2)).astype(jnp.bfloat16)
    grad_cells = lax.all_to_all(grad_out, "chan", split_axis=1, concat_axis=0, tiled=True)
    grad_cube = grad_cells.reshape(filters, row_count // 2, H // 2, W // 2)
    tap_part = jnp.einsum(
        "dqaibje,fqij->abedf", hidden_cube, grad_cube, preferred_element_type=jnp.float32
    )
    tap_part = tap_part.reshape(8, channels, filters)
    tap_owned = lax.psum_scatter(
        spread_blocks(tap_part, space_count, chan_count),
        ("space", "chan"),
        scatter_dimension=0,
        tiled=True,
    )
    dhidden = jnp.einsum(
        "abedf,fqij->dqaibje", tap_weights, grad_cube, preferred_element_type=jnp.float32
    )
    dhidden = dhidden.reshape(channels, row_count, H * W)
    pre_grad = gelu_back(dhidden)[0].astype(jnp.bfloat16)
    point_part = jnp.einsum("crp,drp->cd", inputs, pre_grad, preferred_element_type=jnp.float32)
    d_acts = jnp.einsum(
        "cd,drp->crp", w_point, pre_grad, preferred_element_type=jnp.float32
    ).astype(jnp.bfloat16)
    point_blocks = spread_blocks(point_part.reshape(1, channels, channels), space_count, chan_count)
    point_owned = lax.psum_scatter(point_blocks, ("space", "chan"), scatter_dimension=0, tiled=True)
    d_point = point_owned.reshape(channels // chan_count, channels // space_count) * in_scale
    d_tap = tap_owned.reshape(8, channels // chan_count, filters // space_count) * out_scale
    return (out_map, d_acts, d_point, d_tap)


def solution(mesh):
    placed = (P("chan", "space", None), P(), P(), P("chan", "space", None))
    return jax.shard_map(
        shards,
        mesh=mesh,
        in_specs=placed,
        out_specs=(
            P(None, ("space", "chan"), None),
            P(None, ("space", "chan"), None),
            P("chan", "space"),
            P(None, "chan", "space"),
        ),
        check_vma=False,
    )
```

profile of v0, /device:TPU:29, one launch (start us, length us, event | category | flops | bytes accessed | tf_op | source)
XLA Modules:
  0.0 580.4 jit_solution(10632524823051007500)
XLA Ops:
  7.2 2.9 copy.58
  10.0 6.4 %all-to-all-start.1 = ((bf16[16,32,1024]{2,0,1:T(8,128)(2,1)}), bf16[16,32,1024]{2,0,1:T(8,128)(2,1)S(1)}, u32[]{:S(2)}, u32[]{:S(2)}) async-start(bf16[16,32,1024]{2,0,1:T(8,128)(2,1)} %copy.58), calls=%async_computation.1 | async-start | bytes 2097152 | tf_op jit(solution)/shard_map/all_to_all | solution.py:46
  16.4 11.4 %copy.53 = bf16[16,64,4096]{2,0,1:T(8,128)(2,1)} copy(bf16[16,64,4096]{2,1,0:T(8,128)(2,1)} %param.4) | data formatting | bytes 16777216 | tf_op args[0]
  27.8 12.0 %all-to-all-done.1 = bf16[16,32,1024]{2,0,1:T(8,128)(2,1)S(1)} async-done(((bf16[16,32,1024]{2,0,1:T(8,128)(2,1)}), bf16[16,32,1024]{2,0,1:T(8,128)(2,1)S(1)}, u32[]{:S(2)}, u32[]{:S(2)}) %all-to-all-start.1) | async-done | bytes 1048608 | tf_op jit(solution)/shard_map/all_to_all | solution.py:46
  39.8 5.5 all-to-all-start
  45.2 0.2 reduce-scatter.3.cloned.1.call-start
  45.5 0.1 copy.99
  45.6 4.3 reshape.37
  49.9 12.0 %convolution_bitcast_fusion = f32[256,2,2,32,2,32,2]{0,5,6,4,2,3,1:T(8,128)S(1)} fusion(bf16[2,2,2,256,256,1,1]{4,3,2,1,0,6,5:T(8,128)(2,1)S(1)} %bitcast.69, bf16[256,2,32,32,1,1,1]{3,2,0,1,6,5,4:T(8,128)(2,1)} %bitcast.70), kind=kOutput, calls=%fused_computation.15 | convolution fusion | flops 2147483648 | bytes 18874368 | tf_op jit(solution)/shard_map/abedf,fqij->dqaibje/dot_general | solution.py:58
  61.9 13.4 %copy.61 = f32[256,2,2,32,2,32,2]{0,6,5,4,3,2,1:T(2,128)} copy(f32[256,2,2,32,2,32,2]{0,5,6,4,2,3,1:T(8,128)S(1)} %convolution_bitcast_fusion) | data formatting | bytes 33554432 | tf_op jit(solution)/shard_map/abedf,fqij->dqaibje/transpose | solution.py:58
  75.3 20.5 %reshape.38 = f32[256,4,4096]{0,2,1:T(8,128)} reshape(f32[256,2,2,32,2,32,2]{0,6,5,4,3,2,1:T(2,128)} %copy.61) | data formatting | bytes 33554432 | tf_op jit(solution)/shard_map/reshape | solution.py:61
  95.8 17.5 %copy.62 = f32[256,4,4096]{2,0,1:T(8,128)} copy(f32[256,4,4096]{0,2,1:T(8,128)} %reshape.38) | data formatting | bytes 33554432 | tf_op jit(solution)/shard_map/reshape | solution.py:61
  113.3 116.9 %all-to-all-done = bf16[16,64,4096]{2,0,1:T(8,128)(2,1)} async-done(((bf16[16,64,4096]{2,0,1:T(8,128)(2,1)}), bf16[16,64,4096]{2,0,1:T(8,128)(2,1)}, u32[]{:S(2)}, u32[]{:S(2)}) %all-to-all-start) | async-done | bytes 8388640 | tf_op jit(solution)/shard_map/all_to_all | solution.py:30
  230.2 7.9 %copy.54 = bf16[16,16,4,4096]{3,0,1,2:T(8,128)(2,1)} copy(bf16[16,16,4,4096]{3,0,2,1:T(8,128)(2,1)} %bitcast.1) | data formatting | bytes 16777216 | tf_op jit(solution)/shard_map/all_to_all | solution.py:30
  238.1 22.1 %fusion.6 = (bf16[256,4,4096]{2,0,1:T(8,128)(2,1)}, bf16[256,4,4096]{2,0,1:T(8,128)(2,1)}) fusion(f32[256,4,4096]{2,0,1:T(8,128)} %copy.62, bf16[256,4,4096]{2,0,1:T(8,128)(2,1)} %bitcast.72, bf16[256,256]{1,0:T(8,128)(2,1)S(1)} %copy-done.1), kind=kOutput, calls=%fused_computation.8 | convolution fusion | flops 2239758336 | bytes 42074112 | tf_op jit(solution)/shard_map/cd,crp->drp/dot_general | solution.py:37
  260.2 8.1 %convolution_bitcast_fusion.1 = f32[256,256]{0,1:T(8,128)S(1)} fusion(bf16[256,4,4096]{2,0,1:T(8,128)(2,1)} %get-tuple-element.20, bf16[256,4,4096]{2,0,1:T(8,128)(2,1)} %bitcast.73), kind=kOutput, calls=%fused_computation.20 | convolution fusion | flops 2147483648 | bytes 17039360 | tf_op jit(solution)/shard_map/crp,drp->cd/dot_general | solution.py:63
  268.3 11.9 %copy.56 = bf16[256,4,4096]{0,2,1:T(8,128)(2,1)} copy(bf16[256,4,4096]{2,0,1:T(8,128)(2,1)} %get-tuple-element.21) | data formatting | bytes 16777216 | tf_op jit(solution)/shard_map/convert_element_type | solution.py:39
  280.3 13.1 %reshape.35 = bf16[256,2,2,32,2,32,2]{0,6,5,4,3,2,1:T(2,128)(2,1)} reshape(bf16[256,4,4096]{0,2,1:T(8,128)(2,1)} %copy.56) | data formatting | bytes 16777216 | tf_op jit(solution)/shard_map/reshape | solution.py:40
  293.4 0.1 copy.65
  293.5 0.1 reshape_reshape.6
  293.7 0.7 copy.66
  294.5 13.9 %fusion.15 = f32[2,2,2,256,256]{4,3,2,1,0:T(8,128)} fusion(bf16[256,2,32,32,1,1,1]{3,2,0,1,6,5,4:T(8,128)(2,1)} %bitcast.71, bf16[256,2,2,32,2,32,2]{0,6,5,4,3,2,1:T(2,128)(2,1)} %reshape.35), kind=kOutput, calls=%fused_computation.19 | convolution fusion | flops 2147483648 | bytes 11534336 | tf_op jit(solution)/shard_map/dqaibje,fqij->abedf/dot_general | solution.py:48
  308.4 2.3 reshape_reshape.7
  310.7 1.6 copy.69
  312.3 5.7 bitcast_convert_fusion
  318.1 2.1 copy.70
  320.2 9.0 %convert_bitcast_fusion = bf16[256,4,4096]{0,2,1:T(8,128)(2,1)} fusion(bf16[256,4,4096]{2,0,1:T(8,128)(2,1)} %get-tuple-element.20, bf16[256,256]{1,0:T(8,128)(2,1)S(1)} %copy-done.1), kind=kOutput, calls=%fused_computation.14 | convolution fusion | flops 2151677952 | bytes 16908288 | tf_op jit(solution)/shard_map/cd,drp->crp/dot_general | solution.py:64
  329.2 14.5 %copy.71 = bf16[256,4,4096]{2,1,0:T(4,128)(2,1)} copy(bf16[256,4,4096]{0,2,1:T(8,128)(2,1)} %convert_bitcast_fusion) | data formatting | bytes 16777216
  343.8 87.0 %reduce-scatter.3.cloned.1.call-done = f32[1,1,16,128]{3,2,0,1:T(8,128)} async-done(((f32[32,1,16,128]{3,2,0,1:T(8,128)}), f32[1,1,16,128]{3,2,0,1:T(8,128)}) %reduce-scatter.3.cloned.1.call-update) | async-done | bytes 8208 | tf_op jit(solution)/shard_map/reduce_scatter | solution.py:68
  430.7 1.3 multiply_bitcast_fusion.1
  432.0 140.0 %reduce-scatter.5.cloned.1.call-done = f32[1,8,16,128]{3,2,1,0:T(8,128)} async-done(((f32[32,8,16,128]{3,2,1,0:T(8,128)}), f32[1,8,16,128]{3,2,1,0:T(8,128)}) %reduce-scatter.5.cloned.1.call-update) | async-done | bytes 65552 | tf_op jit(solution)/shard_map/reduce_scatter | solution.py:52
  572.1 1.5 multiply_bitcast_fusion
  (7 shorter events, 0.1 us)
Async XLA Ops:
  7.2 42.7 %copy-start = (bf16[8,256,256]{2,1,0:T(8,128)(2,1)S(1)}, bf16[8,256,256]{2,1,0:T(8,128)(2,1)}, u32[]{:S(2)}) copy-start(bf16[8,256,256]{2,1,0:T(8,128)(2,1)} %param.6) | copy-start | bytes 3145732
  10.0 29.7 %all-to-all-start.1 = ((bf16[16,32,1024]{2,0,1:T(8,128)(2,1)}), bf16[16,32,1024]{2,0,1:T(8,128)(2,1)S(1)}, u32[]{:S(2)}, u32[]{:S(2)}) async-start(bf16[16,32,1024]{2,0,1:T(8,128)(2,1)} %copy.58), calls=%async_computation.1 | async-start | bytes 2097152 | tf_op jit(solution)/shard_map/all_to_all | solution.py:46
  39.8 190.4 %all-to-all-start = ((bf16[16,64,4096]{2,0,1:T(8,128)(2,1)}), bf16[16,64,4096]{2,0,1:T(8,128)(2,1)}, u32[]{:S(2)}, u32[]{:S(2)}) async-start(bf16[16,64,4096]{2,0,1:T(8,128)(2,1)} %copy.53), calls=%async_computation | async-start | bytes 16777216 | tf_op jit(solution)/shard_map/all_to_all | solution.py:30
  45.2 385.5 %reduce-scatter.3.cloned.1.call-start = ((), (), s32[]{:S(2)}) async-start(), calls=%async_computation.4 | async-start | bytes 270336 | tf_op jit(solution)/shard_map/reduce_scatter | solution.py:68
  230.2 7.9 %copy-start.1 = (bf16[256,256]{1,0:T(8,128)(2,1)S(1)}, bf16[256,256]{1,0:T(8,128)(2,1)}, u32[]{:S(2)}) copy-start(bf16[256,256]{1,0:T(8,128)(2,1)} %param.5) | copy-start | bytes 393220
  294.4 277.7 %reduce-scatter.5.cloned.1.call-start = ((), (), s32[]{:S(2)}) async-start(), calls=%async_computation.5 | async-start | bytes 2162688 | tf_op jit(solution)/shard_map/reduce_scatter | solution.py:52
Sparse Core Ops, SparseCore 0:
  294.5 136.1 reduce-scatter.2
  433.1 138.9 reduce-scatter.4
where the time goes:
time: 588 us; the launch traced here: 580 us
  waiting for transfers between devices  356 us (61%)
  local copies, waits for them, and re-layouts  125 us (21%)
  matrix products  70.9 us (12%)
  between operations  14.1 us (2%)
  starting transfers between devices  12.1 us (2%)
    reduce_scatter x1, waiting for transfers between devices, shards(): lax.psum_scatter(spread_blocks(tap_part, space_count, chan_count), ('spac...  140 us
    all_to_all x1, waiting for transfers between devices, shards(): lax.all_to_all(acts, 'chan', split_axis=1, concat_axis=0, tiled=True)  117 us
    reduce_scatter x1, waiting for transfers between devices, shards(): lax.psum_scatter(point_blocks, ('space', 'chan'), scatter_dimension=0, ti...  87 us
    reshape x2, local copies, waits for them, and re-layouts, shards(): dhidden = dhidden.reshape(channels, row_count, H * W)  38 us
    unnamed x8, local copies, waits for them, and re-layouts  30.9 us
    dot_general x1, matrix products, shards(): jnp.einsum('cd,crp->drp', w_point, inputs, preferred_element_type=jnp.flo...  22.1 us
    dot_general x1, matrix products, shards(): jnp.einsum('dqaibje,fqij->abedf', hidden_cube, grad_cube, preferred_eleme...  13.9 us
    transpose x1, local copies, waits for them, and re-layouts, shards(): jnp.einsum('abedf,fqij->dqaibje', tap_weights, grad_cube, preferred_eleme...  13.4 us
  transfers between devices with their start and end apart: 4, of which 4 were waited for; matrix products, arithmetic and copies ran while one was open for 22% of the time, Pallas kernels for 0%

commit v1 on v0

v1 whole, which is shorter than its diff:
```python
import functools
import math

import jax
import jax.numpy as jnp
from jax import lax
from jax.experimental import pallas as pl
from jax.experimental.pallas import tpu as pltpu
from jax.sharding import PartitionSpec as P

H = 64
W = 64
BLOCK = 8 * W
CHUNK = 2 * BLOCK
ROOT = math.sqrt(2.0 / math.pi)
CUBIC = 0.044715


def dot(a, b):
    return lax.dot_general(a, b, (((1,), (0,)), ((), ())), preferred_element_type=jnp.float32)


def dot_nt(a, b):
    return lax.dot_general(a, b, (((1,), (1,)), ((), ())), preferred_element_type=jnp.float32)


def tap_order(position):
    quarter = BLOCK // 4
    u = position // quarter
    rest = position % quarter
    i = rest // (W // 2)
    j = rest % (W // 2)
    return (2 * i + u // 2) * W + 2 * j + u % 2


def kernel(
    spaces, chans, planes, in_scale, out_scale,
    xs, gs, wp, wt,
    out_o, da_o, dtap_o, dpoint_o,
    recv, recvg, acc, recv_a, send_b, recv_b, taps, dtaps, order, back, wt_t, wp_t,
    send_sem, g_send, recv_sem, g_recv, a_send, a_recv, b_send, b_recv,
):
    me_s, me_c = lax.axis_index("space"), lax.axis_index("chan")
    width = xs.shape[1]
    pairs = planes // 2
    parts = xs.shape[2] // CHUNK
    out_cells = CHUNK // 4
    filters = acc.shape[3]

    barrier = pltpu.get_barrier_semaphore()
    for o in range(1, chans):
        pl.semaphore_signal(barrier, inc=1, device_id={"chan": lax.rem(me_c + o, chans)})
    for o in range(1, spaces):
        pl.semaphore_signal(barrier, inc=1, device_id={"space": lax.rem(me_s + o, spaces)})
    pl.semaphore_wait(barrier, chans + spaces - 2)

    mine = pl.ds(pl.multiple_of(me_c * width, width), width)

    def remote(src, dst, ssem, rsem, device):
        return pltpu.make_async_remote_copy(
            src_ref=src, dst_ref=dst, send_sem=ssem, recv_sem=rsem, device_id=device)

    def g_block(peer):
        return gs.at[pl.ds(peer * pairs, pairs)]

    def x_block(peer, k):
        lanes = pl.ds(pl.multiple_of((k % parts) * CHUNK, CHUNK), CHUNK)
        return xs.at[pl.ds(peer * planes + 2 * (k // parts), 2), :, lanes]

    pltpu.make_async_copy(g_block(me_c), recvg.at[:, mine], g_recv).start()

    @pl.loop(1, chans)
    def _(o):
        peer = lax.rem(me_c + o, chans)
        remote(g_block(peer), recvg.at[:, mine], g_send, g_recv, {"chan": peer}).start()

    @pl.loop(0, pairs * parts)
    def _(k):
        pltpu.make_async_copy(x_block(me_c, k), recv.at[k, :, mine], recv_sem.at[k]).start()

        @pl.loop(1, chans)
        def _(o):
            peer = lax.rem(me_c + o, chans)
            remote(x_block(peer, k), recv.at[k, :, mine], send_sem, recv_sem.at[k], {"chan": peer}).start()

    acc[...] = jnp.zeros_like(acc)
    rows = lax.broadcasted_iota(jnp.int32, (BLOCK, BLOCK), 0)
    cols = lax.broadcasted_iota(jnp.int32, (BLOCK, BLOCK), 1)
    order[...] = jnp.where(rows == tap_order(cols), 1.0, 0.0).astype(jnp.bfloat16)
    back[...] = jnp.where(cols == tap_order(rows), 1.0, 0.0).astype(jnp.bfloat16)
    wp_t[...] = wp[...].astype(jnp.float32).T.astype(jnp.bfloat16)

    @pl.loop(0, 8)
    def _(t):
        wt_t[t] = wt[t].astype(jnp.float32).T.astype(jnp.bfloat16)

    def add_term(slot, term):
        for s in range(spaces):
            acc[s, slot] += term[:, s * filters:(s + 1) * filters]

    pltpu.make_async_copy(recvg, recvg, g_recv).wait()

    @pl.loop(0, pairs * parts)
    def _(k):
        pltpu.make_async_copy(recv.at[k], recv.at[k], recv_sem.at[k]).wait()
        q, part = k // parts, k % parts
        quarter = BLOCK // 4
        for a in range(2):
            for h in range(2):
                moved = dot(recv[k, a, :, h * BLOCK:(h + 1) * BLOCK], order[...]).astype(jnp.bfloat16)
                for u in range(4):
                    taps[4 * a + u, :, h * quarter:(h + 1) * quarter] = moved[:, u * quarter:(u + 1) * quarter]
        g_lanes = pl.ds(pl.multiple_of(part * out_cells, out_cells), out_cells)
        g = recvg[q, :, g_lanes]
        out = jnp.zeros((wt.shape[2], out_cells), jnp.float32)
        for t in range(8):
            x = taps[t]
            pre = dot(wp_t[...], x)
            dh = dot(wt[t], g)
            square = pre * pre
            th = jnp.tanh(ROOT * pre * (1.0 + CUBIC * square))
            half = 0.5 * (1.0 + th)
            hidden = (pre * half).astype(jnp.bfloat16)
            slope = half + (0.5 * ROOT) * pre * (1.0 - th * th) * (1.0 + 3.0 * CUBIC * square)
            grad = (dh * slope).astype(jnp.bfloat16)
            out += dot(wt_t[t], hidden)
            add_term(t, dot_nt(hidden, g))
            add_term(8, dot_nt(x, grad))
            d_in = dot(wp[...], grad).astype(jnp.bfloat16)
            for h in range(2):
                dtaps[t // 4, h, :, (t % 4) * quarter:(t % 4 + 1) * quarter] = d_in[:, h * quarter:(h + 1) * quarter]
        out_o[q, :, g_lanes] = out.astype(jnp.bfloat16)
        for a in range(2):
            for h in range(2):
                lanes = pl.ds(pl.multiple_of(part * CHUNK + h * BLOCK, BLOCK), BLOCK)
                da_o[2 * q + a, :, lanes] = dot(dtaps[a, h], back[...]).astype(jnp.bfloat16)

    copies = []
    for o in range(1, spaces):
        other = lax.rem(me_s + o, spaces)
        copy = remote(acc.at[other], recv_a.at[me_s], a_send.at[o - 1], a_recv.at[o - 1], {"space": other})
        copy.start()
        copies.append(copy)
    for copy in copies:
        copy.wait()

    def reduced(c):
        at = pl.ds(pl.multiple_of(c * width, width), width)
        total = acc[me_s, :, at, :]
        for o in range(1, spaces):
            total += recv_a[lax.rem(me_s + o, spaces), :, at, :]
        return total.astype(jnp.bfloat16)

    @pl.loop(1, chans)
    def _(o):
        peer = lax.rem(me_c + o, chans)
        send_b[peer] = reduced(peer)
        remote(send_b.at[peer], recv_b.at[me_c], b_send, b_recv, {"chan": peer}).start()

    send_b[me_c] = reduced(me_c)
    pltpu.make_async_copy(send_b.at[me_c], recv_b.at[me_c], b_recv).start()
    pltpu.make_async_copy(recv_b, recv_b, b_recv).wait()
    total = recv_b[0].astype(jnp.float32)
    for c in range(1, chans):
        total += recv_b[c].astype(jnp.float32)
    dtap_o[...] = total[:8] * out_scale
    dpoint_o[...] = total[8] * in_scale

    sent = xs.at[pl.ds(0, planes * (chans - 1))]
    pltpu.make_async_copy(sent, sent, send_sem).wait()
    sent_g = gs.at[pl.ds(0, pairs * (chans - 1))]
    pltpu.make_async_copy(sent_g, sent_g, g_send).wait()
    sent_b = send_b.at[pl.ds(0, chans - 1)]
    pltpu.make_async_copy(sent_b, sent_b, b_send).wait()


def shards(acts, w_point, w_tap, grad_out):
    spaces = lax.axis_size("space")
    chans = lax.axis_size("chan")
    width, rows, cells = acts.shape
    planes = rows // chans
    channels = width * chans
    filters = w_tap.shape[2]
    in_cells = rows * spaces * H * W
    xs = jnp.transpose(acts, (1, 0, 2))
    gs = jnp.transpose(grad_out, (1, 0, 2))
    chunks = (planes // 2) * (cells // CHUNK)
    bf16, f32 = jnp.bfloat16, jnp.float32
    vmem = pl.BlockSpec(memory_space=pltpu.VMEM)
    own = filters // spaces
    out, da, d_tap, d_point = pl.pallas_call(
        functools.partial(kernel, spaces, chans, planes, 1.0 / math.sqrt(in_cells), 1.0 / math.sqrt(in_cells // 8)),
        out_shape=(
            jax.ShapeDtypeStruct((planes // 2, filters, cells // 4), bf16),
            jax.ShapeDtypeStruct((planes, channels, cells), bf16),
            jax.ShapeDtypeStruct((8, width, own), f32),
            jax.ShapeDtypeStruct((width, own), f32),
        ),
        in_specs=[pl.BlockSpec(memory_space=pl.ANY)] * 2 + [vmem] * 2,
        out_specs=(vmem,) * 4,
        scratch_shapes=[
            pltpu.VMEM((chunks, 2, channels, CHUNK), bf16),
            pltpu.VMEM((planes // 2, filters, cells // 4), bf16),
            pltpu.VMEM((spaces, 9, channels, own), f32),
            pltpu.VMEM((spaces, 9, channels, own), f32),
            pltpu.VMEM((chans, 9, width, own), bf16),
            pltpu.VMEM((chans, 9, width, own), bf16),
            pltpu.VMEM((8, channels, CHUNK // 4), bf16),
            pltpu.VMEM((2, 2, channels, BLOCK), bf16),
            pltpu.VMEM((BLOCK, BLOCK), bf16),
            pltpu.VMEM((BLOCK, BLOCK), bf16),
            pltpu.VMEM((8, filters, channels), bf16),
            pltpu.VMEM((channels, channels), bf16),
            pltpu.SemaphoreType.DMA,
            pltpu.SemaphoreType.DMA,
            pltpu.SemaphoreType.DMA((chunks,)),
            pltpu.SemaphoreType.DMA,
            pltpu.SemaphoreType.DMA((max(spaces - 1, 1),)),
            pltpu.SemaphoreType.DMA((max(spaces - 1, 1),)),
            pltpu.SemaphoreType.DMA,
            pltpu.SemaphoreType.DMA,
        ],
        compiler_params=pltpu.CompilerParams(
            collective_id=0, has_side_effects=True, vmem_limit_bytes=58 * 2**20
        ),
        cost_estimate=pl.CostEstimate(flops=24 * 10**9, bytes_accessed=30 * 10**6, transcendentals=4 * 10**6),
    )(xs, gs, w_point, w_tap)
    return (jnp.transpose(out, (1, 0, 2)), jnp.transpose(da, (1, 0, 2)), d_point, d_tap)


def solution(mesh):
    placed = (P("chan", "space", None), P(), P(), P("chan", "space", None))
    return jax.shard_map(
        shards,
        mesh=mesh,
        in_specs=placed,
        out_specs=(
            P(None, ("space", "chan"), None),
            P(None, ("space", "chan"), None),
            P("chan", "space"),
            P(None, "chan", "space"),
        ),
        check_vma=False,
    )
```

time: 588 us -> 266 us (0.45); the launches traced: 580 us -> 266 us
  waiting for transfers between devices: 356 us -> 0 us
  Pallas kernels: 0 us -> 235 us
  local copies, waits for them, and re-layouts: 125 us -> 30.8 us
  matrix products: 70.9 us -> 0 us
  between operations: 14.1 us -> 0.64 us
  starting transfers between devices: 12.1 us -> 0 us
    pallas_call x0 -> x1, Pallas kernels: none -> 235 us  [shards(): pl.pallas_call(functools.partial(kernel, spaces, chans, planes, 1.0 / mat...]
    reduce_scatter x2 -> x0, waiting for transfers between devices: 227 us -> none  [the longest x1 140 us: shards(): lax.psum_scatter(spread_blocks(tap_part, space_count, chan_count), ('spac...]
    all_to_all x2 -> x0, waiting for transfers between devices: 129 us -> none  [the longest x1 117 us: shards(): lax.all_to_all(acts, 'chan', split_axis=1, concat_axis=0, tiled=True)]
    dot_general x6 -> x0, matrix products: 70.9 us -> none  [the longest x1 22.1 us: shards(): jnp.einsum('cd,crp->drp', w_point, inputs, preferred_element_type=jnp.flo...]
    reshape x4 -> x0, local copies, waits for them, and re-layouts: 55.5 us -> none  [the longest x2 38 us: shards(): dhidden = dhidden.reshape(channels, row_count, H * W)]
    transpose x3 -> x0, local copies, waits for them, and re-layouts: 15.7 us -> none  [the longest x1 13.4 us: shards(): jnp.einsum('abedf,fqij->dqaibje', tap_weights, grad_cube, preferred_eleme...]
    convert_element_type x1 -> x0, local copies, waits for them, and re-layouts: 11.9 us -> none  [shards(): hidden = hidden_full.astype(jnp.bfloat16)]
    all_to_all x2 -> x0, starting transfers between devices: 11.8 us -> none  [the longest x1 6.38 us: shards(): lax.all_to_all(grad_out, 'chan', split_axis=1, concat_axis=0, tiled=True)]
  transfers between devices with their start and end apart: 4 -> 0, of which waited for: 4 -> 0; matrix products, arithmetic and copies ran while one was open for 22% -> 0% of each run, Pallas kernels for 0% -> 0%
where the time goes in v1:
time: 266 us
  Pallas kernels  235 us (88%)
  local copies, waits for them, and re-layouts  30.8 us (12%)
    pallas_call x1, Pallas kernels, shards(): pl.pallas_call(functools.partial(kernel, spaces, chans, planes, 1.0 / mat...  235 us
    unnamed x10, local copies, waits for them, and re-layouts  30.8 us

profile of v1, /device:TPU:29, one launch (start us, length us, event | category | flops | bytes accessed | tf_op | source)
XLA Modules:
  0.0 266.0 jit_solution(3127447339859337905)
XLA Ops:
  0.6 2.8 %copy.15 = bf16[16,32,1024]{2,0,1:T(8,128)(2,1)} copy(bf16[16,32,1024]{2,1,0:T(8,128)(2,1)} %param.7) | data formatting | bytes 2097152 | tf_op args[3]
  3.4 11.4 %copy.14 = bf16[16,64,4096]{2,0,1:T(8,128)(2,1)} copy(bf16[16,64,4096]{2,1,0:T(8,128)(2,1)} %param.4) | data formatting | bytes 16777216 | tf_op args[0]
  14.8 234.6 %shard_map.75 = (bf16[2,256,1024]{2,1,0:T(8,128)(2,1)}, bf16[4,256,4096]{2,1,0:T(8,128)(2,1)}, f32[8,16,128]{2,1,0:T(8,128)}, f32[16,128]{1,0:T(8,128)}) custom-call(bf16[64,16,4096]{2,1,0:T(8,128)(2,1)} %bitcast.9, bf16[32,16,1024]{2,1,0:T(8,128)(2,1)} %bitcast.11, bf16[256,256]{1,0:T(8,128)(2,1)} %wp.1, bf16[8,256,256]{2,1,0:T(8,128)(2,1)} %wt.1), custom_call_target="tpu_custom_call" | custom-call | flops 24000000000 | bytes 30000000 | tf_op jit(solution)/shard_map/pallas_call | solution.py:191
  249.4 3.3 %copy.10 = bf16[256,2,1024]{2,1,0:T(2,128)(2,1)} copy(bf16[256,2,1024]{2,0,1:T(8,128)(2,1)} %bitcast.10) | data formatting | bytes 2097152
  252.6 0.0 copy-start.1
  252.6 0.0 copy-start
  252.6 12.2 %copy.11 = bf16[256,4,4096]{2,1,0:T(4,128)(2,1)} copy(bf16[256,4,4096]{2,0,1:T(8,128)(2,1)} %bitcast.8) | data formatting | bytes 16777216
  264.8 0.0 copy-done.1
  264.8 0.6 copy.18
  265.4 0.0 copy-done
  265.4 0.6 copy.19
Async XLA Ops:
  252.6 12.2 %copy-start.1 = (f32[16,128]{1,0:T(8,128)S(1)}, f32[16,128]{1,0:T(8,128)}, u32[]{:S(2)}) copy-start(f32[16,128]{1,0:T(8,128)} %get-tuple-element.22) | copy-start | bytes 24580
  252.6 12.8 %copy-start = (f32[8,16,128]{2,1,0:T(8,128)S(1)}, f32[8,16,128]{2,1,0:T(8,128)}, u32[]{:S(2)}) copy-start(f32[8,16,128]{2,1,0:T(8,128)} %get-tuple-element.23) | copy-start | bytes 196612

commit v2 on v1

--- a/solution.py
+++ b/solution.py
@@ -35,15 +35,33 @@
 
 def kernel(
     spaces, chans, planes, in_scale, out_scale,
-    xs, gs, wp, wt,
+    acts, grad_out, wp, wt,
     out_o, da_o, dtap_o, dpoint_o,
-    recv, recvg, acc, recv_a, send_b, recv_b, taps, dtaps, order, back, wt_t, wp_t,
-    send_sem, g_send, recv_sem, g_recv, a_send, a_recv, b_send, b_recv,
+    xs, gs, stage, g_stage, da_v,
+    recv, recvg, acc, recv_a, send_b, recv_b, taps, dtaps, grads, hid, order, back, wt_t, wp_t,
+    load_sem, g_load, da_sem, send_sem, g_send, recv_sem, g_recv, a_send, a_recv, b_send, b_recv,
 ):
     me_s, me_c = lax.axis_index("space"), lax.axis_index("chan")
-    width = xs.shape[1]
+    width = acts.shape[0]
     pairs = planes // 2
-    parts = xs.shape[2] // CHUNK
+    parts = acts.shape[2] // CHUNK
+
+    def load(part, slot):
+        lanes = pl.ds(pl.multiple_of(part * CHUNK, CHUNK), CHUNK)
+        return pltpu.make_async_copy(acts.at[:, :, lanes], stage.at[slot], load_sem.at[slot])
+
+    g_copy = pltpu.make_async_copy(grad_out, g_stage, g_load)
+    g_copy.start()
+    load(0, 0).start()
+
+    def swap(src, dst):
+        @pl.loop(0, src.shape[2] // 128)
+        def _(lane):
+            lanes = pl.ds(pl.multiple_of(lane * 128, 128), 128)
+            for r in range(0, src.shape[1], 16):
+                piece = src[:, r:r + 16, lanes].astype(jnp.float32)
+                dst[r:r + 16, :, lanes] = jnp.swapaxes(piece, 0, 1).astype(jnp.bfloat16)
+
     out_cells = CHUNK // 4
     filters = acc.shape[3]
 
@@ -64,9 +82,10 @@
         return gs.at[pl.ds(peer * pairs, pairs)]
 
     def x_block(peer, k):
-        lanes = pl.ds(pl.multiple_of((k % parts) * CHUNK, CHUNK), CHUNK)
-        return xs.at[pl.ds(peer * planes + 2 * (k // parts), 2), :, lanes]
-
+        return xs.at[k // pairs, pl.ds(peer * planes + 2 * (k % pairs), 2)]
+
+    g_copy.wait()
+    swap(g_stage, gs)
     pltpu.make_async_copy(g_block(me_c), recvg.at[:, mine], g_recv).start()
 
     @pl.loop(1, chans)
@@ -74,14 +93,26 @@
         peer = lax.rem(me_c + o, chans)
         remote(g_block(peer), recvg.at[:, mine], g_send, g_recv, {"chan": peer}).start()
 
-    @pl.loop(0, pairs * parts)
-    def _(k):
-        pltpu.make_async_copy(x_block(me_c, k), recv.at[k, :, mine], recv_sem.at[k]).start()
-
-        @pl.loop(1, chans)
-        def _(o):
-            peer = lax.rem(me_c + o, chans)
-            remote(x_block(peer, k), recv.at[k, :, mine], send_sem, recv_sem.at[k], {"chan": peer}).start()
+    @pl.loop(0, parts)
+    def _(part):
+        slot = part % 2
+
+        @pl.when(part + 1 < parts)
+        def _():
+            load(part + 1, (part + 1) % 2).start()
+
+        load(part, slot).wait()
+        swap(stage.at[slot], xs.at[part])
+
+        @pl.loop(0, pairs)
+        def _(q):
+            k = part * pairs + q
+            pltpu.make_async_copy(x_block(me_c, k), recv.at[k, :, mine], recv_sem.at[k]).start()
+
+            @pl.loop(1, chans)
+            def _(o):
+                peer = lax.rem(me_c + o, chans)
+                remote(x_block(peer, k), recv.at[k, :, mine], send_sem, recv_sem.at[k], {"chan": peer}).start()
 
     acc[...] = jnp.zeros_like(acc)
     rows = lax.broadcasted_iota(jnp.int32, (BLOCK, BLOCK), 0)
@@ -92,7 +123,7 @@
 
     @pl.loop(0, 8)
     def _(t):
-        wt_t[t] = wt[t].astype(jnp.float32).T.astype(jnp.bfloat16)
+        wt_t[:, pl.ds(pl.multiple_of(t * wp.shape[0], 128), wp.shape[0])] = wt[t].astype(jnp.float32).T.astype(jnp.bfloat16)
 
     def add_term(slot, term):
         for s in range(spaces):
@@ -103,18 +134,19 @@
     @pl.loop(0, pairs * parts)
     def _(k):
         pltpu.make_async_copy(recv.at[k], recv.at[k], recv_sem.at[k]).wait()
-        q, part = k // parts, k % parts
+        q, part = k % pairs, k // pairs
         quarter = BLOCK // 4
         for a in range(2):
             for h in range(2):
                 moved = dot(recv[k, a, :, h * BLOCK:(h + 1) * BLOCK], order[...]).astype(jnp.bfloat16)
                 for u in range(4):
-                    taps[4 * a + u, :, h * quarter:(h + 1) * quarter] = moved[:, u * quarter:(u + 1) * quarter]
+                    at = (4 * a + u) * out_cells + h * quarter
+                    taps[:, at:at + quarter] = moved[:, u * quarter:(u + 1) * quarter]
         g_lanes = pl.ds(pl.multiple_of(part * out_cells, out_cells), out_cells)
         g = recvg[q, :, g_lanes]
-        out = jnp.zeros((wt.shape[2], out_cells), jnp.float32)
         for t in range(8):
-            x = taps[t]
+            here = slice(t * out_cells, (t + 1) * out_cells)
+            x = taps[:, here]
             pre = dot(wp_t[...], x)
             dh = dot(wt[t], g)
             square = pre * pre
@@ -123,17 +155,20 @@
             hidden = (pre * half).astype(jnp.bfloat16)
             slope = half + (0.5 * ROOT) * pre * (1.0 - th * th) * (1.0 + 3.0 * CUBIC * square)
             grad = (dh * slope).astype(jnp.bfloat16)
-            out += dot(wt_t[t], hidden)
+            hid[t * hidden.shape[0]:(t + 1) * hidden.shape[0], :] = hidden
+            grads[:, here] = grad
             add_term(t, dot_nt(hidden, g))
-            add_term(8, dot_nt(x, grad))
             d_in = dot(wp[...], grad).astype(jnp.bfloat16)
             for h in range(2):
                 dtaps[t // 4, h, :, (t % 4) * quarter:(t % 4 + 1) * quarter] = d_in[:, h * quarter:(h + 1) * quarter]
-        out_o[q, :, g_lanes] = out.astype(jnp.bfloat16)
+        add_term(8, dot_nt(taps[...], grads[...]))
+        out_o[q, :, g_lanes] = dot(wt_t[...], hid[...]).astype(jnp.bfloat16)
         for a in range(2):
             for h in range(2):
                 lanes = pl.ds(pl.multiple_of(part * CHUNK + h * BLOCK, BLOCK), BLOCK)
-                da_o[2 * q + a, :, lanes] = dot(dtaps[a, h], back[...]).astype(jnp.bfloat16)
+                da_v[2 * q + a, :, lanes] = dot(dtaps[a, h], back[...]).astype(jnp.bfloat16)
+        block = (pl.ds(2 * q, 2), slice(None), pl.ds(pl.multiple_of(part * CHUNK, CHUNK), CHUNK))
+        pltpu.make_async_copy(da_v.at[block], da_o.at[block], da_sem).start()
 
     copies = []
     for o in range(1, spaces):
@@ -166,10 +201,11 @@
     dtap_o[...] = total[:8] * out_scale
     dpoint_o[...] = total[8] * in_scale
 
-    sent = xs.at[pl.ds(0, planes * (chans - 1))]
+    sent = xs.at[:, pl.ds(0, planes * (chans - 1))]
     pltpu.make_async_copy(sent, sent, send_sem).wait()
     sent_g = gs.at[pl.ds(0, pairs * (chans - 1))]
     pltpu.make_async_copy(sent_g, sent_g, g_send).wait()
+    pltpu.make_async_copy(da_v, da_o, da_sem).wait()
     sent_b = send_b.at[pl.ds(0, chans - 1)]
     pltpu.make_async_copy(sent_b, sent_b, b_send).wait()
 
@@ -182,8 +218,6 @@
     channels = width * chans
     filters = w_tap.shape[2]
     in_cells = rows * spaces * H * W
-    xs = jnp.transpose(acts, (1, 0, 2))
-    gs = jnp.transpose(grad_out, (1, 0, 2))
     chunks = (planes // 2) * (cells // CHUNK)
     bf16, f32 = jnp.bfloat16, jnp.float32
     vmem = pl.BlockSpec(memory_space=pltpu.VMEM)
@@ -197,20 +231,30 @@
             jax.ShapeDtypeStruct((width, own), f32),
         ),
         in_specs=[pl.BlockSpec(memory_space=pl.ANY)] * 2 + [vmem] * 2,
-        out_specs=(vmem,) * 4,
+        out_specs=(vmem, pl.BlockSpec(memory_space=pl.ANY), vmem, vmem),
         scratch_shapes=[
+            pltpu.VMEM((cells // CHUNK, rows, width, CHUNK), bf16),
+            pltpu.VMEM((rows // 2, width, cells // 4), bf16),
+            pltpu.VMEM((2, width, rows, CHUNK), bf16),
+            pltpu.VMEM((width, rows // 2, cells // 4), bf16),
+            pltpu.VMEM((planes, channels, cells), bf16),
             pltpu.VMEM((chunks, 2, channels, CHUNK), bf16),
             pltpu.VMEM((planes // 2, filters, cells // 4), bf16),
             pltpu.VMEM((spaces, 9, channels, own), f32),
             pltpu.VMEM((spaces, 9, channels, own), f32),
             pltpu.VMEM((chans, 9, width, own), bf16),
             pltpu.VMEM((chans, 9, width, own), bf16),
-            pltpu.VMEM((8, channels, CHUNK // 4), bf16),
+            pltpu.VMEM((channels, 2 * CHUNK), bf16),
             pltpu.VMEM((2, 2, channels, BLOCK), bf16),
+            pltpu.VMEM((channels, 2 * CHUNK), bf16),
+            pltpu.VMEM((8 * channels, CHUNK // 4), bf16),
             pltpu.VMEM((BLOCK, BLOCK), bf16),
             pltpu.VMEM((BLOCK, BLOCK), bf16),
-            pltpu.VMEM((8, filters, channels), bf16),
+            pltpu.VMEM((filters, 8 * channels), bf16),
             pltpu.VMEM((channels, channels), bf16),
+            pltpu.SemaphoreType.DMA((2,)),
+            pltpu.SemaphoreType.DMA,
+            pltpu.SemaphoreType.DMA,
             pltpu.SemaphoreType.DMA,
             pltpu.SemaphoreType.DMA,
             pltpu.SemaphoreType.DMA((chunks,)),
@@ -224,7 +268,7 @@
             collective_id=0, has_side_effects=True, vmem_limit_bytes=58 * 2**20
         ),
         cost_estimate=pl.CostEstimate(flops=24 * 10**9, bytes_accessed=30 * 10**6, transcendentals=4 * 10**6),
-    )(xs, gs, w_point, w_tap)
+    )(acts, grad_out, w_point, w_tap)
     return (jnp.transpose(out, (1, 0, 2)), jnp.transpose(da, (1, 0, 2)), d_point, d_tap)
 
 

time: 266 us -> 250 us (0.940)
  local copies, waits for them, and re-layouts: 30.8 us -> 16.7 us
  Pallas kernels: 235 us -> 232 us
    unnamed x10 -> x8, local copies, waits for them, and re-layouts: 30.8 us -> 16.7 us
where the time goes in v2:
time: 250 us
  Pallas kernels  232 us (93%)
  local copies, waits for them, and re-layouts  16.7 us (7%)
    pallas_call x1, Pallas kernels, shards(): pl.pallas_call(functools.partial(kernel, spaces, chans, planes, 1.0 / mat...  232 us
    unnamed x8, local copies, waits for them, and re-layouts  16.7 us

profile of v2, /device:TPU:29, one launch (start us, length us, event | category | flops | bytes accessed | tf_op | source)
XLA Modules:
  0.0 249.7 jit_solution(10093523300979678553)
XLA Ops:
  0.6 232.4 %shard_map.75 = (bf16[2,256,1024]{2,1,0:T(8,128)(2,1)}, bf16[4,256,4096]{2,1,0:T(8,128)(2,1)}, f32[8,16,128]{2,1,0:T(8,128)}, f32[16,128]{1,0:T(8,128)}) custom-call(bf16[16,64,4096]{2,1,0:T(8,128)(2,1)} %acts.1, bf16[16,32,1024]{2,1,0:T(8,128)(2,1)} %grad_out.1, bf16[256,256]{1,0:T(8,128)(2,1)} %wp.1, bf16[8,256,256]{2,1,0:T(8,128)(2,1)} %wt.1), custom_call_target="tpu_custom_call" | custom-call | flops 24000000000 | bytes 30000000 | tf_op jit(solution)/shard_map/pallas_call | solution.py:225
  233.0 3.3 %copy.8 = bf16[256,2,1024]{2,1,0:T(2,128)(2,1)} copy(bf16[256,2,1024]{2,0,1:T(8,128)(2,1)} %bitcast.3) | data formatting | bytes 2097152
  236.3 0.0 copy-start.1
  236.3 0.0 copy-start
  236.3 12.2 %copy.9 = bf16[256,4,4096]{2,1,0:T(4,128)(2,1)} copy(bf16[256,4,4096]{2,0,1:T(8,128)(2,1)} %bitcast.2) | data formatting | bytes 16777216
  248.5 0.0 copy-done.1
  248.5 0.6 copy.12
  249.1 0.0 copy-done
  249.1 0.6 copy.13
Async XLA Ops:
  236.3 12.2 %copy-start.1 = (f32[16,128]{1,0:T(8,128)S(1)}, f32[16,128]{1,0:T(8,128)}, u32[]{:S(2)}) copy-start(f32[16,128]{1,0:T(8,128)} %get-tuple-element.22) | copy-start | bytes 24580
  236.3 12.8 %copy-start = (f32[8,16,128]{2,1,0:T(8,128)S(1)}, f32[8,16,128]{2,1,0:T(8,128)}, u32[]{:S(2)}) copy-start(f32[8,16,128]{2,1,0:T(8,128)} %get-tuple-element.23) | copy-start | bytes 196612

commit v3 on v2

--- a/solution.py
+++ b/solution.py
@@ -44,6 +44,7 @@
     me_s, me_c = lax.axis_index("space"), lax.axis_index("chan")
     width = acts.shape[0]
     pairs = planes // 2
+    stride = next(n for n in range(chans // 2 - 1, 0, -1) if math.gcd(n, chans) == 1)
     parts = acts.shape[2] // CHUNK
 
     def load(part, slot):
@@ -111,7 +112,7 @@
 
             @pl.loop(1, chans)
             def _(o):
-                peer = lax.rem(me_c + o, chans)
+                peer = lax.rem(me_c + stride * o, chans)
                 remote(x_block(peer, k), recv.at[k, :, mine], send_sem, recv_sem.at[k], {"chan": peer}).start()
 
     acc[...] = jnp.zeros_like(acc)

time: 250 us -> 250 us (level)
  no operation moved by 1% of the time
where the time goes in v3:
time: 250 us; the launch traced here: 249 us
  Pallas kernels  232 us (93%)
  local copies, waits for them, and re-layouts  16.7 us (7%)
    pallas_call x1, Pallas kernels, shards(): pl.pallas_call(functools.partial(kernel, spaces, chans, planes, 1.0 / mat...  232 us
    unnamed x8, local copies, waits for them, and re-layouts  16.7 us

profile of v3, /device:TPU:29, one launch (start us, length us, event | category | flops | bytes accessed | tf_op | source)
XLA Modules:
  0.0 249.1 jit_solution(1862500131538711117)
XLA Ops:
  0.6 231.8 %shard_map.75 = (bf16[2,256,1024]{2,1,0:T(8,128)(2,1)}, bf16[4,256,4096]{2,1,0:T(8,128)(2,1)}, f32[8,16,128]{2,1,0:T(8,128)}, f32[16,128]{1,0:T(8,128)}) custom-call(bf16[16,64,4096]{2,1,0:T(8,128)(2,1)} %acts.1, bf16[16,32,1024]{2,1,0:T(8,128)(2,1)} %grad_out.1, bf16[256,256]{1,0:T(8,128)(2,1)} %wp.1, bf16[8,256,256]{2,1,0:T(8,128)(2,1)} %wt.1), custom_call_target="tpu_custom_call" | custom-call | flops 24000000000 | bytes 30000000 | tf_op jit(solution)/shard_map/pallas_call | solution.py:226
  232.4 3.3 %copy.8 = bf16[256,2,1024]{2,1,0:T(2,128)(2,1)} copy(bf16[256,2,1024]{2,0,1:T(8,128)(2,1)} %bitcast.3) | data formatting | bytes 2097152
  235.7 0.0 copy-start.1
  235.7 0.0 copy-start
  235.7 12.2 %copy.9 = bf16[256,4,4096]{2,1,0:T(4,128)(2,1)} copy(bf16[256,4,4096]{2,0,1:T(8,128)(2,1)} %bitcast.2) | data formatting | bytes 16777216
  247.8 0.0 copy-done.1
  247.9 0.6 copy.12
  248.4 0.0 copy-done
  248.5 0.6 copy.13
Async XLA Ops:
  235.7 12.2 %copy-start.1 = (f32[16,128]{1,0:T(8,128)S(1)}, f32[16,128]{1,0:T(8,128)}, u32[]{:S(2)}) copy-start(f32[16,128]{1,0:T(8,128)} %get-tuple-element.22) | copy-start | bytes 24580
  235.7 12.8 %copy-start = (f32[8,16,128]{2,1,0:T(8,128)S(1)}, f32[8,16,128]{2,1,0:T(8,128)}, u32[]{:S(2)}) copy-start(f32[8,16,128]{2,1,0:T(8,128)} %get-tuple-element.23) | copy-start | bytes 196612

commit v4 on v2

--- a/solution.py
+++ b/solution.py
@@ -37,7 +37,7 @@
     spaces, chans, planes, in_scale, out_scale,
     acts, grad_out, wp, wt,
     out_o, da_o, dtap_o, dpoint_o,
-    xs, gs, stage, g_stage, da_v,
+    xs, gs, stage, g_stage, da_v, da_p,
     recv, recvg, acc, recv_a, send_b, recv_b, taps, dtaps, grads, hid, order, back, wt_t, wp_t,
     load_sem, g_load, da_sem, send_sem, g_send, recv_sem, g_recv, a_send, a_recv, b_send, b_recv,
 ):
@@ -53,6 +53,10 @@
     g_copy = pltpu.make_async_copy(grad_out, g_stage, g_load)
     g_copy.start()
     load(0, 0).start()
+
+    def leave(part, slot):
+        lanes = pl.ds(pl.multiple_of(part * CHUNK, CHUNK), CHUNK)
+        return pltpu.make_async_copy(da_v.at[slot], da_o.at[:, :, lanes], da_sem.at[slot])
 
     def swap(src, dst):
         @pl.loop(0, src.shape[2] // 128)
@@ -165,10 +169,24 @@
         out_o[q, :, g_lanes] = dot(wt_t[...], hid[...]).astype(jnp.bfloat16)
         for a in range(2):
             for h in range(2):
-                lanes = pl.ds(pl.multiple_of(part * CHUNK + h * BLOCK, BLOCK), BLOCK)
-                da_v[2 * q + a, :, lanes] = dot(dtaps[a, h], back[...]).astype(jnp.bfloat16)
-        block = (pl.ds(2 * q, 2), slice(None), pl.ds(pl.multiple_of(part * CHUNK, CHUNK), CHUNK))
-        pltpu.make_async_copy(da_v.at[block], da_o.at[block], da_sem).start()
+                da_p[2 * q + a, :, h * BLOCK:(h + 1) * BLOCK] = dot(dtaps[a, h], back[...]).astype(jnp.bfloat16)
+
+        @pl.when(q == pairs - 1)
+        def _():
+            slot = part % 2
+
+            @pl.when(part >= 2)
+            def _():
+                leave(part - 2, slot).wait()
+
+            @pl.loop(0, CHUNK // 128)
+            def _(lane):
+                lanes = pl.ds(pl.multiple_of(lane * 128, 128), 128)
+                for c in range(0, da_p.shape[1], 64):
+                    piece = da_p[:, c:c + 64, lanes].astype(jnp.float32)
+                    da_v[slot, c:c + 64, :, lanes] = jnp.swapaxes(piece, 0, 1).astype(jnp.bfloat16)
+
+            leave(part, slot).start()
 
     copies = []
     for o in range(1, spaces):
@@ -205,7 +223,8 @@
     pltpu.make_async_copy(sent, sent, send_sem).wait()
     sent_g = gs.at[pl.ds(0, pairs * (chans - 1))]
     pltpu.make_async_copy(sent_g, sent_g, g_send).wait()
-    pltpu.make_async_copy(da_v, da_o, da_sem).wait()
+    for part in range(max(parts - 2, 0), parts):
+        leave(part, part % 2).wait()
     sent_b = send_b.at[pl.ds(0, chans - 1)]
     pltpu.make_async_copy(sent_b, sent_b, b_send).wait()
 
@@ -226,7 +245,7 @@
         functools.partial(kernel, spaces, chans, planes, 1.0 / math.sqrt(in_cells), 1.0 / math.sqrt(in_cells // 8)),
         out_shape=(
             jax.ShapeDtypeStruct((planes // 2, filters, cells // 4), bf16),
-            jax.ShapeDtypeStruct((planes, channels, cells), bf16),
+            jax.ShapeDtypeStruct((channels, planes, cells), bf16),
             jax.ShapeDtypeStruct((8, width, own), f32),
             jax.ShapeDtypeStruct((width, own), f32),
         ),
@@ -237,7 +256,8 @@
             pltpu.VMEM((rows // 2, width, cells // 4), bf16),
             pltpu.VMEM((2, width, rows, CHUNK), bf16),
             pltpu.VMEM((width, rows // 2, cells // 4), bf16),
-            pltpu.VMEM((planes, channels, cells), bf16),
+            pltpu.VMEM((2, channels, planes, CHUNK), bf16),
+            pltpu.VMEM((planes, channels, CHUNK), bf16),
             pltpu.VMEM((chunks, 2, channels, CHUNK), bf16),
             pltpu.VMEM((planes // 2, filters, cells // 4), bf16),
             pltpu.VMEM((spaces, 9, channels, own), f32),
@@ -254,7 +274,7 @@
             pltpu.VMEM((channels, channels), bf16),
             pltpu.SemaphoreType.DMA((2,)),
             pltpu.SemaphoreType.DMA,
-            pltpu.SemaphoreType.DMA,
+            pltpu.SemaphoreType.DMA((2,)),
             pltpu.SemaphoreType.DMA,
             pltpu.SemaphoreType.DMA,
             pltpu.SemaphoreType.DMA((chunks,)),
@@ -269,7 +289,7 @@
         ),
         cost_estimate=pl.CostEstimate(flops=24 * 10**9, bytes_accessed=30 * 10**6, transcendentals=4 * 10**6),
     )(acts, grad_out, w_point, w_tap)
-    return (jnp.transpose(out, (1, 0, 2)), jnp.transpose(da, (1, 0, 2)), d_point, d_tap)
+    return (jnp.transpose(out, (1, 0, 2)), da, d_point, d_tap)
 
 
 def solution(mesh):

time: 250 us -> 248 us (level)
  local copies, waits for them, and re-layouts: 16.7 us -> 13 us
    unnamed x8, local copies, waits for them, and re-layouts: 16.7 us -> 13 us
where the time goes in v4:
time: 248 us; the launch traced here: 247 us
  Pallas kernels  234 us (94%)
  local copies, waits for them, and re-layouts  13 us (5%)
    pallas_call x1, Pallas kernels, shards(): pl.pallas_call(functools.partial(kernel, spaces, chans, planes, 1.0 / mat...  234 us
    unnamed x8, local copies, waits for them, and re-layouts  13 us

profile of v4, /device:TPU:29, one launch (start us, length us, event | category | flops | bytes accessed | tf_op | source)
XLA Modules:
  0.0 247.2 jit_solution(18030334361954152138)
XLA Ops:
  0.6 233.5 %shard_map.75 = (bf16[2,256,1024]{2,1,0:T(8,128)(2,1)}, bf16[256,4,4096]{2,1,0:T(4,128)(2,1)}, f32[8,16,128]{2,1,0:T(8,128)}, f32[16,128]{1,0:T(8,128)}) custom-call(bf16[16,64,4096]{2,1,0:T(8,128)(2,1)} %acts.1, bf16[16,32,1024]{2,1,0:T(8,128)(2,1)} %grad_out.1, bf16[256,256]{1,0:T(8,128)(2,1)} %wp.1, bf16[8,256,256]{2,1,0:T(8,128)(2,1)} %wt.1), custom_call_target="tpu_custom_call" | custom-call | flops 24000000000 | bytes 30000000 | tf_op jit(solution)/shard_map/pallas_call | solution.py:244
  234.2 3.3 %copy.8 = bf16[256,2,1024]{2,1,0:T(2,128)(2,1)} copy(bf16[256,2,1024]{2,0,1:T(8,128)(2,1)} %bitcast.1) | data formatting | bytes 2097152
  237.4 0.0 copy-start.1
  237.4 0.0 copy-start
  237.4 8.5 %copy.12 = bf16[256,4,4096]{2,1,0:T(4,128)(2,1)} copy(bf16[256,4,4096]{2,1,0:T(4,128)(2,1)} %get-tuple-element.21) | data formatting | bytes 16777216
  246.0 0.0 copy-done.1
  246.0 0.6 copy.13
  246.6 0.0 copy-done
  246.6 0.6 copy.14
Async XLA Ops:
  237.4 8.5 %copy-start.1 = (f32[16,128]{1,0:T(8,128)S(1)}, f32[16,128]{1,0:T(8,128)}, u32[]{:S(2)}) copy-start(f32[16,128]{1,0:T(8,128)} %get-tuple-element.22) | copy-start | bytes 24580
  237.4 9.1 %copy-start = (f32[8,16,128]{2,1,0:T(8,128)S(1)}, f32[8,16,128]{2,1,0:T(8,128)}, u32[]{:S(2)}) copy-start(f32[8,16,128]{2,1,0:T(8,128)} %get-tuple-element.23) | copy-start | bytes 196612
